TPU v7x, 256 devices: a whole 4x4x8 slice. The times are simulated.
256 devices in a mesh: node: 32 (over z, x_hi, core), local: 8 (over y, x_lo).
Axes of the slice: x: 4 (x_hi: 2, x_lo: 2; x = x_hi * 2 + x_lo), y: 4, z: 8, core: 2. Of those that a mesh axis runs over, the one named last changes fastest.
Arguments:
- inputs: bfloat16 [131072, 4096], P(('node', 'local')), may hold values from -24 to 24
- cotangent: bfloat16 [131072, 1024], P(('node', 'local')), may hold values from -6 to 6
- weight: bfloat16 [4096, 1024], P(('node', 'local')), may hold values from -0.1875 to 0.1875
Outputs:
- grad_weight: float32 [2048, 2048], P(('node', 'local'))
- grad_input: bfloat16 [131072, 4096], P(('node', 'local'))
All inputs are finite; a program needn't handle non-finite values.
Results may differ from a plain program's by a relative error of at most 0.03.
Values may be sent and summed in bfloat16 or wider, within the bound.
A program may use at most 128 MiB of HBM per device.

v0:
```python
import math

import jax
import jax.numpy as jnp
from jax import lax
from jax.sharding import PartitionSpec as P

QBLOCK = 2048


EPS_FLOOR = 1e-06
LEVELS = 127.0


def encode(values):
    scales = ((jnp.max(jnp.abs(values), axis=-1) + EPS_FLOOR) / LEVELS).astype(jnp.bfloat16)
    ratio = values / scales.astype(jnp.float32)[..., None]
    block_codes = jnp.clip(jnp.floor(ratio + 0.5), -LEVELS, LEVELS).astype(jnp.bfloat16)
    return (block_codes, scales)


def restore_sum(block_codes, scales, axis_dim):
    return jnp.sum(
        block_codes.astype(jnp.float32) * scales.astype(jnp.float32)[..., None], axis=axis_dim
    )


def local(inputs, cotangent, weight):
    node_count = lax.axis_size("node")
    local_count = lax.axis_size("local")
    in_width = inputs.shape[1]
    out_width = cotangent.shape[1]
    unscale = 1.0 / math.sqrt(inputs.shape[0] * node_count * local_count)
    own_blocks = in_width * out_width // (QBLOCK * node_count * local_count)
    term = (
        lax.dot_general(
            inputs, cotangent, (((0,), (0,)), ((), ())), preferred_element_type=jnp.float32
        )
        * unscale
    )
    block_codes, scales = encode(term.reshape(node_count, local_count, own_blocks, QBLOCK))
    codes_node, scales_node = (
        lax.all_to_all(block_codes, "local", split_axis=1, concat_axis=1, tiled=True),
        lax.all_to_all(scales, "local", split_axis=1, concat_axis=1, tiled=True),
    )
    first_sum = restore_sum(codes_node, scales_node, 1)
    codes_next, scales_next = encode(first_sum)
    codes_owner, scales_owner = (
        lax.all_to_all(codes_next, "node", split_axis=0, concat_axis=0, tiled=True),
        lax.all_to_all(scales_next, "node", split_axis=0, concat_axis=0, tiled=True),
    )
    grad_weight = restore_sum(codes_owner, scales_owner, 0)
    grad_input = lax.dot_general(
        cotangent,
        lax.all_gather(weight, ("node", "local"), axis=0, tiled=True),
        (((1,), (1,)), ((), ())),
        preferred_element_type=jnp.float32,
    )
    return (grad_weight, grad_input.astype(jnp.bfloat16))


def solution(mesh):
    in_specs = (P(("node", "local"), None), P(("node", "local"), None), P(("node", "local"), None))
    out_specs = (P(("node", "local"), None), P(("node", "local"), None))
    return jax.shard_map(local, mesh=mesh, in_specs=in_specs, out_specs=out_specs, check_vma=False)
```

profile of v0, /device:TPU:1, one launch (start us, length us, event | category | flops | bytes accessed | tf_op | source)
XLA Modules:
  0.0 805.5 jit_solution(16105832218243377657)
XLA Ops:
  7.2 0.0 copy-start
  7.2 0.0 all-gather.2.cloned.1.call-start
  7.2 0.7 all-gather.2.cloned.1.call-update
  7.9 0.5 copy-done
  8.4 10.4 %broadcast_multiply_fusion = f32[4096,1024]{1,0:T(8,128)} fusion(bf16[512,4096]{1,0:T(8,128)(2,1)} %param.3, bf16[512,1024]{1,0:T(8,128)(2,1)S(1)} %copy-done), kind=kOutput, calls=%fused_computation.7 | convolution fusion | flops 4299161600 | bytes 22020096 | tf_op jit(solution)/shard_map/dot_general | solution.py:36
  18.8 19.2 %reshape.47 = f32[32,8,8,2048]{3,2,1,0:T(8,128)} reshape(f32[4096,1024]{1,0:T(8,128)} %broadcast_multiply_fusion) | data formatting | bytes 33554432 | tf_op jit(solution)/shard_map/reshape | solution.py:41
  38.0 7.1 abs_reduce_fusion
  45.1 0.1 copy.25
  45.2 0.7 reshape.49
  45.9 5.9 all-to-all-start.1
  51.8 0.1 copy.26
  51.9 10.2 %fusion.3 = bf16[32,8,8,2048]{3,2,0,1:T(8,128)(2,1)} fusion(f32[32,8,8,2048]{3,2,1,0:T(8,128)} %reshape.47, f32[32,8,8]{2,0,1:T(8,128)S(1)} %copy.26), kind=kLoop, calls=%fused_computation.6 | loop fusion | flops 20971520 | bytes 25174016 | tf_op jit(solution)/shard_map/convert_element_type | solution.py:18
  62.1 0.0 all-to-all-done.1
  62.1 5.1 all-to-all-start
  67.2 0.1 reshape.50
  67.3 0.1 copy.28
  67.4 96.2 %all-to-all-done = bf16[32,8,8,2048]{3,2,0,1:T(8,128)(2,1)} async-done(((bf16[32,8,8,2048]{3,2,0,1:T(8,128)(2,1)}), bf16[32,8,8,2048]{3,2,0,1:T(8,128)(2,1)}, u32[]{:S(2)}, u32[]{:S(2)}) %all-to-all-start) | async-done | bytes 8388640 | tf_op jit(solution)/shard_map/all_to_all | solution.py:43
  163.6 5.2 multiply_reduce_fusion
  168.8 0.2 abs_reduce_fusion.1
  169.0 0.1 copy.29
  169.1 0.1 copy.30
  169.2 0.7 copy.31
  169.9 12.0 %all-to-all-start.3 = ((bf16[32,1,8]{2,1,0:T(2,128)(2,1)}), bf16[32,1,8]{2,1,0:T(2,128)(2,1)S(1)}, u32[]{:S(2)}, u32[]{:S(2)}) async-start(bf16[32,1,8]{2,1,0:T(2,128)(2,1)} %copy.31), calls=%async_computation.3 | async-start | bytes 32768 | tf_op jit(solution)/shard_map/all_to_all | solution.py:50
  181.9 1.4 clamp_convert_fusion
  183.3 7.9 all-to-all-done.3
  191.2 4.2 all-to-all-start.2
  195.4 29.6 %all-to-all-done.2 = bf16[32,8,2048]{2,1,0:T(8,128)(2,1)S(1)} async-done(((bf16[32,8,2048]{2,1,0:T(8,128)(2,1)}), bf16[32,8,2048]{2,1,0:T(8,128)(2,1)S(1)}, u32[]{:S(2)}, u32[]{:S(2)}) %all-to-all-start.2) | async-done | bytes 1048608 | tf_op jit(solution)/shard_map/all_to_all | solution.py:49
  225.0 0.9 multiply_reduce_fusion.1
  225.9 563.3 %all-gather.2.cloned.1.call-done = bf16[4096,1024]{1,0:T(8,128)(2,1)} async-done(((bf16[16,1024]{1,0:T(8,128)(2,1)}), bf16[4096,1024]{1,0:T(8,128)(2,1)}) %all-gather.2.cloned.1.call-update) | async-done | bytes 8388624 | tf_op jit(solution)/shard_map/all_gather | solution.py:55
  789.2 9.5 %convolution_convert_fusion = bf16[512,4096]{1,0:T(8,128)(2,1)} fusion(bf16[512,1024]{1,0:T(8,128)(2,1)S(1)} %copy-done, bf16[4096,1024]{1,0:T(8,128)(2,1)} %all-gather.2.cloned.1.call-done), kind=kOutput, calls=%fused_computation.8 | convolution fusion | flops 4297064448 | bytes 13631488 | tf_op jit(solution)/shard_map/dot_general | solution.py:53
  (4 shorter events, 0.1 us)
Async XLA Ops:
  7.2 1.2 copy-start
  7.2 782.0 %all-gather.2.cloned.1.call-start = ((), (), s32[]{:S(2)}) async-start(), calls=%async_computation.4 | async-start | bytes 8421376 | tf_op jit(solution)/shard_map/all_gather | solution.py:55
  45.9 16.2 %all-to-all-start.1 = ((bf16[8,2,128]{2,1,0:T(2,128)(2,1)}), bf16[8,2,128]{2,1,0:T(2,128)(2,1)S(1)}, u32[]{:S(2)}, u32[]{:S(2)}) async-start(bf16[8,2,128]{2,1,0:T(2,128)(2,1)} %reshape.49), calls=%async_computation.1 | async-start | bytes 8192 | tf_op jit(solution)/shard_map/all_to_all | solution.py:44
  62.1 101.5 %all-to-all-start = ((bf16[32,8,8,2048]{3,2,0,1:T(8,128)(2,1)}), bf16[32,8,8,2048]{3,2,0,1:T(8,128)(2,1)}, u32[]{:S(2)}, u32[]{:S(2)}) async-start(bf16[32,8,8,2048]{3,2,0,1:T(8,128)(2,1)} %fusion.3), calls=%async_computation | async-start | bytes 16777216 | tf_op jit(solution)/shard_map/all_to_all | solution.py:43
  169.9 21.3 %all-to-all-start.3 = ((bf16[32,1,8]{2,1,0:T(2,128)(2,1)}), bf16[32,1,8]{2,1,0:T(2,128)(2,1)S(1)}, u32[]{:S(2)}, u32[]{:S(2)}) async-start(bf16[32,1,8]{2,1,0:T(2,128)(2,1)} %copy.31), calls=%async_computation.3 | async-start | bytes 32768 | tf_op jit(solution)/shard_map/all_to_all | solution.py:50
  191.2 33.8 %all-to-all-start.2 = ((bf16[32,8,2048]{2,1,0:T(8,128)(2,1)}), bf16[32,8,2048]{2,1,0:T(8,128)(2,1)S(1)}, u32[]{:S(2)}, u32[]{:S(2)}) async-start(bf16[32,8,2048]{2,1,0:T(8,128)(2,1)} %clamp_convert_fusion), calls=%async_computation.2 | async-start | bytes 2097152 | tf_op jit(solution)/shard_map/all_to_all | solution.py:49
Sparse Core Ops, SparseCore 0:
  9.9 779.2 all-gather.1
where the time goes:
time: 820 us; the launch traced here: 806 us
  waiting for transfers between devices  698 us (85%)
  starting transfers between devices  27.3 us (3%)
  other arithmetic  25 us (3%)
  local copies, waits for them, and re-layouts  21.6 us (3%)
  matrix products  19.8 us (2%)
  between operations  14.1 us (2%)
    all_gather x1, waiting for transfers between devices, local(): lax.all_gather(weight, ('node', 'local'), axis=0, tiled=True)  563 us
    all_to_all x1, waiting for transfers between devices, local(): lax.all_to_all(block_codes, 'local', split_axis=1, concat_axis=1, tiled=T...  96.2 us
    all_to_all x1, waiting for transfers between devices, local(): lax.all_to_all(codes_next, 'node', split_axis=0, concat_axis=0, tiled=True)  29.6 us
    reshape x1, local copies, waits for them, and re-layouts, local(): term.reshape(node_count, local_count, own_blocks, QBLOCK)  19.2 us
  transfers between devices with their start and end apart: 5, of which 4 were waited for; matrix products, arithmetic and copies ran while one was open for 7% of the time, Pallas kernels for 0%

commit v1 on v0

v1 whole, which is shorter than its diff:
```python
import math

import jax
import jax.numpy as jnp
from jax import lax
from jax.experimental import pallas as pl
from jax.experimental.pallas import tpu as pltpu
from jax.sharding import PartitionSpec as P

MESH = pl.DeviceIdType.MESH
EPS_FLOOR = 1e-06
LEVELS = 127.0
BF16, F32 = jnp.bfloat16, jnp.float32

Z = 8
Y_FIRST = (3, 3, 3, 3, 2, 2, 2, 0)

EVENTS = (
    "ag1", "L0", "ag2", "L1", "ag3", "L2", "L3", "zf0",
    "YA0", "XA0", "L4", "YA1", "L5", "YA2", "XA1", "YB0", "L6", "zf1", "YA3", "XB0", "L7", "YA4", "XA2", "YB1",
    "YA5", "YB2", "C0", "XA3", "XB1", "zf2", "YA6", "YB3", "XB2", "C1", "D0", "gi0", "gi1", "gi7",
    "XA4", "XB3", "YB4", "C2", "D1", "zf3", "gi2", "gi6", "XA5", "YB5", "XB4", "C3", "D2", "XA6", "YB6", "XB5",
    "C4", "D3", "gi3", "gi5", "zf4", "XA7", "XB6", "C5", "D4", "gi4", "C6", "D5", "XB7", "D6", "E", "C7", "F",
)


def quantize(load, store, rows, unscale):
    top = jnp.abs(load(0))
    for k in range(1, 8):
        top = jnp.maximum(top, jnp.abs(load(k)))
    top = jnp.broadcast_to(jnp.max(top, axis=1, keepdims=True), (rows, 128)) * unscale
    even = lax.broadcasted_iota(jnp.int32, (rows, 128), 0) % 2 == 0
    top = jnp.maximum(top, jnp.where(even, pltpu.roll(top, rows - 1, 0), pltpu.roll(top, 1, 0)))
    scale = ((top + EPS_FLOOR) / LEVELS).astype(BF16).astype(F32)
    inverse = unscale / scale
    for k in range(8):
        code = jnp.clip(jnp.floor(load(k) * inverse + 0.5), -LEVELS, LEVELS)
        store(k, code * scale)


def kernel(unscale, inp, cot_hbm, w_hbm, gw, gi, cot, win, T, R, RB, W, F, G, CB, ZB, EB, XB, GS,
           in_sem, s_sem, r_sem, ag_s, ag_r, z_s, z_r, cx_s, cx_r, g_s, g_r, zs_s, zs_r, xb_s, xb_r, gi_sem):
    node, loc = lax.axis_index("node"), lax.axis_index("local")
    z, xh, c, y, xl = node // 4, (node // 2) % 2, node % 2, loc // 2, loc % 2

    def dev(z=z, xh=xh, c=c, y=y, xl=xl):
        return (z * 4 + xh * 2 + c, y * 2 + xl)

    def up(v, by, n):
        return (v + by + n) % n

    def to(src, dst, send, recv, target):
        return pltpu.make_async_remote_copy(
            src_ref=src, dst_ref=dst, send_sem=send, recv_sem=recv, device_id=target, device_id_type=MESH)

    def slot_z(s):
        return (z + (4 + s // 2 if s % 2 == 0 else (7 - s) // 2)) % 8

    def load_in(s, half):
        start = pl.multiple_of(slot_z(s) * 512 + half * 256, 256)
        return pltpu.make_async_copy(inp.at[:, pl.ds(start, 256)], win.at[s, half], in_sem.at[s, half])

    cot_copy = pltpu.make_async_copy(cot_hbm, cot, in_sem.at[8, 0])
    w_copy = pltpu.make_async_copy(w_hbm, W.at[z, xh, c, y, xl], in_sem.at[8, 1])
    w_copy.start()
    cot_copy.start()
    for s in range(8):
        for half in range(2):
            load_in(s, half).start()

    peers = [dev(y=up(y, 1, 4)), dev(y=up(y, -1, 4)), dev(y=up(y, 2, 4)), dev(xl=1 - xl), dev(c=1 - c),
             dev(z=up(z, 1, 8)), dev(z=up(z, -1, 8)), dev(xh=1 - xh), dev(xh=1 - xh, c=1 - c), dev(xh=1 - xh, xl=1 - xl)]
    barrier = pltpu.get_barrier_semaphore()
    for peer in peers:
        pl.semaphore_signal(barrier, inc=1, device_id=peer, device_id_type=MESH)
    pl.semaphore_wait(barrier, len(peers))

    def f32(ref):
        return ref[...].astype(F32)

    def sigma(s, q):
        return (2 * (q % 2) - 1) * (1 - 2 * (s % 2))

    def y_copy(s, q, k):
        d = sigma(s, q)
        nxt, prv, far = up(y, d, 4), up(y, -d, 4), up(y, 2, 4)
        src, dst, target = ((R.at[s, q, far], RB.at[s, q, 0:2], dev(y=nxt)),
                            (R.at[s, q, prv], RB.at[s, q, 2:4], dev(y=prv)),
                            (R.at[s, q, nxt], RB.at[s, q, 4:6], dev(y=nxt)),
                            (R.at[s, q, y, 1 - xl], RB.at[s, q, 6], dev(xl=1 - xl)))[k]
        return to(src, dst, s_sem.at[s], r_sem.at[s, q, k], target)

    def x_copy(s, q, k):
        d = sigma(s, q)
        nxt, prv, far = up(y, d, 4), up(y, -d, 4), up(y, 2, 4)
        src, dst, target = ((R.at[s, q, :, 1 - xl], RB.at[s, q, 0:4], dev(xl=1 - xl)),
                            (R.at[s, q, far, xl], RB.at[s, q, 4], dev(y=nxt)),
                            (R.at[s, q, prv, xl], RB.at[s, q, 5], dev(y=prv)),
                            (R.at[s, q, nxt, xl], RB.at[s, q, 6], dev(y=nxt)))[k]
        return to(src, dst, s_sem.at[s], r_sem.at[s, q, k], target)

    def each(lo, hi, body):
        def step(q, carry):
            body(q)
            return carry
        if hi > lo:
            lax.fori_loop(lo, hi, step, 0)

    def leaf(s):
        if s == 0:
            cot_copy.wait()
        for half in range(2):
            load_in(s, half).wait()

        def do_half(half):
            T[...] = lax.dot_general(win[s, half], cot[...], (((0,), (0,)), ((), ())), preferred_element_type=F32)

            def block(b):
                rows = pl.ds(pl.multiple_of(b * 64, 64), 64)
                q, pair = half * 2 + b // 2, (b % 2) * 2

                def store(k, value):
                    R[s, q, pl.ds(pair, 2), :, :, k * 128:(k + 1) * 128] = value.astype(BF16).reshape(2, 2, 16, 128)

                quantize(lambda k: T[rows, k * 128:(k + 1) * 128], store, 64, unscale)

            each(0, 4, block)

            def send(q2):
                q = half * 2 + q2

                @pl.when(q < Y_FIRST[s])
                def _():
                    y_copy(s, q, 0).start()
                    y_copy(s, q, 1).start()

                @pl.when(q >= Y_FIRST[s])
                def _():
                    x_copy(s, q, 0).start()

            each(0, 2, send)

        each(0, 2, do_half)

    def y_forward(s):
        def body(q):
            y_copy(s, q, 0).wait_recv()
            own = R.at[s, q, up(y, sigma(s, q), 4)]
            own[...] = (f32(own) + f32(RB.at[s, q, 0:2])).astype(BF16)
            y_copy(s, q, 2).start()
        each(0, Y_FIRST[s], body)

    def y_cross(s):
        def body(q):
            y_copy(s, q, 1).wait_recv()
            y_copy(s, q, 2).wait_recv()
            own = R.at[s, q, y, 1 - xl]
            own[...] = (f32(own) + f32(RB.at[s, q, 3 - xl]) + f32(RB.at[s, q, 5 - xl])).astype(BF16)
            y_copy(s, q, 3).start()
        each(0, Y_FIRST[s], body)

    def x_leaf(s):
        def body(q):
            x_copy(s, q, 0).wait_recv()
            for part, k in ((up(y, 2, 4), 1), (up(y, -sigma(s, q), 4), 2)):
                own = R.at[s, q, part, xl]
                own[...] = (f32(own) + f32(RB.at[s, q, part])).astype(BF16)
                x_copy(s, q, k).start()
        each(Y_FIRST[s], 4, body)

    def x_forward(s):
        def body(q):
            x_copy(s, q, 1).wait_recv()
            part = up(y, sigma(s, q), 4)
            own = R.at[s, q, part, xl]
            own[...] = (f32(own) + f32(RB.at[s, q, part]) + f32(RB.at[s, q, 4])).astype(BF16)
            x_copy(s, q, 3).start()
        each(Y_FIRST[s], 4, body)

    def g_copy(s):
        return to(G.at[s, :, 1 - c], CB.at[s], g_s.at[s], g_r.at[s], dev(c=1 - c))

    last = [(G.at[7, xh, 1 - c], dev(c=1 - c)), (G.at[7, 1 - xh, c], dev(xh=1 - xh)),
            (G.at[7, 1 - xh, 1 - c], dev(xh=1 - xh, c=1 - c)), (EB.at[1 - xh], dev(xh=1 - xh))]

    def last_copy(i):
        return to(last[i][0], XB.at[i], xb_s.at[i], xb_r.at[i], last[i][1])

    def close(s):
        def y_body(q):
            y_copy(s, q, 3).wait_recv()
            F[pl.ds(pl.multiple_of(q * 16, 16), 16), :] = (
                f32(R.at[s, q, y, xl]) + f32(RB.at[s, q, 2 + xl]) + f32(RB.at[s, q, 4 + xl]) + f32(RB.at[s, q, 6]))

        def x_body(q):
            x_copy(s, q, 2).wait_recv()
            x_copy(s, q, 3).wait_recv()
            F[pl.ds(pl.multiple_of(q * 16, 16), 16), :] = (
                f32(R.at[s, q, y, xl]) + f32(RB.at[s, q, y]) + f32(RB.at[s, q, 5]) + f32(RB.at[s, q, 6]))

        each(0, Y_FIRST[s], y_body)
        each(Y_FIRST[s], 4, x_body)

        def store(k, value):
            G[s, :, :, :, k * 128:(k + 1) * 128] = value.astype(BF16).reshape(2, 2, 16, 128)

        quantize(lambda k: F[:, k * 128:(k + 1) * 128], store, 64, 1.0)
        if s < 7:
            g_copy(s).start()
        else:
            for i in range(3):
                last_copy(i).start()

    def z_copy(s, half=0):
        right, left = dev(z=up(z, 1, 8)), dev(z=up(z, -1, 8))
        if s == 0:
            return to(G.at[0, half, c], ZB.at[0, half], zs_s.at[7 * half], zs_r.at[7 * half], left if half else right)
        return to(G.at[s, :, c], ZB.at[s], zs_s.at[s], zs_r.at[s], right if s % 2 else left)

    def pass_on(s):
        g_copy(s).wait_recv()
        if 1 <= s <= 2:
            z_copy(0, s - 1).wait_recv()
        elif s >= 3:
            z_copy(s - 2).wait_recv()
        for half in range(2):
            own = G.at[s, half, c]
            total = f32(own) + f32(CB.at[s, half])
            if s >= 3:
                total = total + f32(ZB.at[s - 2, half])
            elif s - 1 == half:
                total = total + f32(ZB.at[0, half])
            own[...] = total.astype(BF16)
        for half in range(2 if s == 0 else 1):
            z_copy(s, half).start()

    def arrive():
        z_copy(5).wait_recv()
        z_copy(6).wait_recv()
        EB[...] = (f32(ZB.at[5]) + f32(ZB.at[6])).astype(BF16)
        last_copy(3).start()

    def finish():
        for i in range(4):
            last_copy(i).wait_recv()
        total = f32(G.at[7, xh, c]) + f32(ZB.at[5, xh]) + f32(ZB.at[6, xh])
        for i in range(4):
            total = total + f32(XB.at[i])
        gw[...] = total

    def ag1(d):
        piece = W.at[z, xh, c, y, xl]
        return to(piece, piece, ag_s.at[d - 1], ag_r.at[d - 1], dev(y=up(y, d, 4)))

    def ag2():
        piece = W.at[z, xh, c, :, xl]
        return to(piece, piece, ag_s.at[3], ag_r.at[3], dev(xl=1 - xl))

    def ag3():
        piece = W.at[z, xh, c]
        return to(piece, piece, ag_s.at[4], ag_r.at[4], dev(xh=1 - xh, xl=1 - xl))

    def ring(way, k, half):
        d = 1 - 2 * way
        piece = W.at[up(z, -d * (k - 1), 8), half, c]
        i = way * 8 + (k - 1) * 2 + half
        return to(piece, piece, z_s.at[i], z_r.at[i], dev(z=up(z, d, 8)))

    def ring_steps(k):
        return [(way, k, half) for way in range(2) for half in range(2) if k < 4 or half == way]

    def swap(i):
        piece = W.at[up(z, -i, 8), :, c]
        return to(piece, piece, cx_s.at[i], cx_r.at[i], dev(c=1 - c))

    def hop(k):
        if k == 0:
            ag3().wait_recv()
            for args in ring_steps(1):
                ring(*args).start()
            swap(0).start()
            return
        for way, _, half in ring_steps(k):
            ring(way, k, half).wait_recv()
            if k < 4 and (k < 3 or half == way):
                ring(way, k + 1, half).start()
        for i in ((k, 8 - k) if k < 4 else (4,)):
            swap(i).start()

    def put(i, slot):
        start = pl.multiple_of(up(z, -i, 8) * 512, 512)
        return pltpu.make_async_copy(GS.at[slot], gi.at[:, pl.ds(start, 512)], gi_sem.at[slot])

    gi_done = []

    def grad_input(i):
        swap(i).wait_recv()
        slot = len(gi_done) % 2
        if len(gi_done) >= 2:
            put(gi_done[-2], slot).wait()
        rows = W.at[up(z, -i, 8)]

        def column(xh_):
            value = lax.dot_general(cot[...], rows[xh_].reshape(256, 1024), (((1,), (1,)), ((), ())),
                                    preferred_element_type=F32)
            GS[slot, :, pl.ds(pl.multiple_of(xh_ * 256, 256), 256)] = value.astype(BF16)

        each(0, 2, column)
        put(i, slot).start()
        gi_done.append(i)

    def start_ag():
        w_copy.wait()
        for d in (1, 3, 2):
            ag1(d).start()

    def second_ag():
        for d in (1, 3, 2):
            ag1(d).wait_recv()
        ag2().start()

    def third_ag():
        ag2().wait_recv()
        ag3().start()

    single = {"ag1": start_ag, "ag2": second_ag, "ag3": third_ag, "E": arrive, "F": finish}
    numbered = {"L": leaf, "YA": y_forward, "XA": x_leaf, "YB": y_cross, "XB": x_forward, "C": close, "D": pass_on,
                "zf": hop, "gi": grad_input}
    for event in EVENTS:
        if event in single:
            single[event]()
        else:
            numbered[event[:-1]](int(event[-1]))

    for i in gi_done[-2:]:
        put(i, gi_done.index(i) % 2).wait()
    for s in range(8):
        pltpu.make_async_copy(RB.at[s], RB.at[s], s_sem.at[s]).wait()
    for d in (1, 3, 2):
        ag1(d).wait_send()
    ag2().wait_send()
    ag3().wait_send()
    for k in range(1, 5):
        for args in ring_steps(k):
            ring(*args).wait_send()
    for i in range(8):
        swap(i).wait_send()
    for s in range(7):
        g_copy(s).wait_send()
        for half in range(2 if s == 0 else 1):
            z_copy(s, half).wait_send()
    for i in range(4):
        last_copy(i).wait_send()


def local(unscale, inputs, cotangent, weight):
    dma = pltpu.SemaphoreType.DMA
    hbm = pl.BlockSpec(memory_space=pl.ANY)
    grad_weight, grad_input = pl.pallas_call(
        lambda *refs: kernel(unscale, *refs),
        out_shape=(jax.ShapeDtypeStruct((16, 1024), F32), jax.ShapeDtypeStruct((512, 4096), BF16)),
        in_specs=[hbm] * 3,
        out_specs=(pl.BlockSpec(memory_space=pltpu.VMEM), hbm),
        scratch_shapes=[
            pltpu.VMEM((512, 1024), BF16),
            pltpu.VMEM((8, 2, 512, 256), BF16),
            pltpu.VMEM((256, 1024), F32),
            pltpu.VMEM((8, 4, 4, 2, 16, 1024), BF16),
            pltpu.VMEM((8, 4, 7, 16, 1024), BF16),
            pltpu.VMEM((8, 2, 2, 4, 2, 16, 1024), BF16),
            pltpu.VMEM((64, 1024), F32),
            pltpu.VMEM((8, 2, 2, 16, 1024), BF16),
            pltpu.VMEM((7, 2, 16, 1024), BF16),
            pltpu.VMEM((7, 2, 16, 1024), BF16),
            pltpu.VMEM((2, 16, 1024), BF16),
            pltpu.VMEM((4, 16, 1024), BF16),
            pltpu.VMEM((2, 512, 512), BF16),
            dma((9, 2)), dma((8,)), dma((8, 4, 4)),
            dma((5,)), dma((5,)), dma((16,)), dma((16,)), dma((8,)), dma((8,)),
            dma((7,)), dma((7,)), dma((8,)), dma((8,)), dma((4,)), dma((4,)), dma((2,)),
        ],
        compiler_params=pltpu.CompilerParams(collective_id=0, has_side_effects=True, vmem_limit_bytes=48 << 20),
        cost_estimate=pl.CostEstimate(flops=4 * 512 * 4096 * 1024, bytes_accessed=10 << 20, transcendentals=0),
        name="exchange",
    )(inputs, cotangent, weight)
    return grad_weight.reshape(8, 2048), grad_input


def solution(mesh):
    sharded = P(("node", "local"), None)
    tokens = 512 * mesh.shape["node"] * mesh.shape["local"]
    unscale = 1.0 / math.sqrt(tokens)
    return jax.shard_map(lambda *args: local(unscale, *args), mesh=mesh, in_specs=(sharded,) * 3,
                         out_specs=(sharded,) * 2, check_vma=False)
```

time: 820 us -> 103 us (0.13); the launches traced: 806 us -> 103 us
  waiting for transfers between devices: 698 us -> 0 us
  Pallas kernels: 0 us -> 92.8 us
  starting transfers between devices: 27.3 us -> 0 us
  other arithmetic: 25 us -> 0 us
  matrix products: 19.8 us -> 0 us
  between operations: 14.1 us -> 0.66 us
  local copies, waits for them, and re-layouts: 21.6 us -> 9.26 us
    all_gather x1 -> x0, waiting for transfers between devices: 563 us -> none  [local(): lax.all_gather(weight, ('node', 'local'), axis=0, tiled=True)]
    all_to_all x4 -> x0, waiting for transfers between devices: 134 us -> none  [the longest x1 96.2 us: local(): lax.all_to_all(block_codes, 'local', split_axis=1, concat_axis=1, tiled=T...]
    pallas_call x0 -> x1, Pallas kernels: none -> 92.8 us  [local(): pl.pallas_call(lambda *refs: kernel(unscale, *refs), out_shape=(jax.Shape...]
    all_to_all x4 -> x0, starting transfers between devices: 27.3 us -> none  [the longest x1 12 us: local(): lax.all_to_all(scales_next, 'node', split_axis=0, concat_axis=0, tiled=True)]
    dot_general x2 -> x0, matrix products: 19.8 us -> none  [the longest x1 10.4 us: local(): lax.dot_general(inputs, cotangent, (((0,), (0,)), ((), ())), preferred_el...]
    reshape x1, local copies, waits for them, and re-layouts: 19.2 us -> 0.65 us  [local(): return (grad_weight.reshape(8, 2048), grad_input)]
    convert_element_type x5 -> x0, other arithmetic: 11.6 us -> none  [the longest x2 11.6 us: encode(): jnp.clip(jnp.floor(ratio + 0.5), -LEVELS, LEVELS).astype(jnp.bfloat16)]
  transfers between devices with their start and end apart: 5 -> 0, of which waited for: 4 -> 0; matrix products, arithmetic and copies ran while one was open for 7% -> 0% of each run, Pallas kernels for 0% -> 0%
where the time goes in v1:
time: 103 us
  Pallas kernels  92.8 us (90%)
  local copies, waits for them, and re-layouts  9.26 us (9%)
    pallas_call x1, Pallas kernels, local(): pl.pallas_call(lambda *refs: kernel(unscale, *refs), out_shape=(jax.Shape...  92.8 us
    unnamed x7, local copies, waits for them, and re-layouts  8.61 us

profile of v1, /device:TPU:1, one launch (start us, length us, event | category | flops | bytes accessed | tf_op | source)
XLA Modules:
  0.0 102.7 jit_solution(7082986376452518224)
XLA Ops:
  0.6 0.0 copy-start.1
  0.6 1.2 %copy-done.1 = bf16[512,1024]{1,0:T(8,128)(2,1)S(1)} copy-done((bf16[512,1024]{1,0:T(8,128)(2,1)S(1)}, bf16[512,1024]{1,0:T(8,128)(2,1)}, u32[]{:S(2)}) %copy-start.1) | copy-done | bytes 1048600
  1.9 0.0 copy-start.2
  1.9 0.8 copy-done.2
  2.6 92.8 %exchange.1 = (f32[16,1024]{1,0:T(8,128)S(1)}, bf16[512,4096]{1,0:T(8,128)(2,1)S(1)}) custom-call(bf16[512,4096]{1,0:T(8,128)(2,1)} %refs_0_.1, bf16[512,1024]{1,0:T(8,128)(2,1)S(1)} %copy-done.1, bf16[16,1024]{1,0:T(8,128)(2,1)S(1)} %copy-done.2), custom_call_target="tpu_custom_call" | custom-call | flops 8589934592 | bytes 10485760 | tf_op jit(solution)/shard_map/exchange/pallas_call | solution.py:359
  95.4 0.0 copy-start
  95.5 1.9 %copy-done = bf16[512,4096]{1,0:T(8,128)(2,1)} copy-done((bf16[512,4096]{1,0:T(8,128)(2,1)}, bf16[512,4096]{1,0:T(8,128)(2,1)S(1)}, u32[]{:S(2)}) %copy-start) | copy-done | bytes 4194328
  97.4 0.7 reshape.7
  98.0 4.7 %copy.6 = bf16[512,4096]{1,0:T(8,128)(2,1)} copy(bf16[512,4096]{1,0:T(8,128)(2,1)} %copy-done) | data formatting | bytes 8388608
Async XLA Ops:
  0.6 1.2 %copy-start.1 = (bf16[512,1024]{1,0:T(8,128)(2,1)S(1)}, bf16[512,1024]{1,0:T(8,128)(2,1)}, u32[]{:S(2)}) copy-start(bf16[512,1024]{1,0:T(8,128)(2,1)} %refs_1_.1) | copy-start | bytes 3145732
  1.9 0.8 copy-start.2
  95.4 1.9 %copy-start = (bf16[512,4096]{1,0:T(8,128)(2,1)}, bf16[512,4096]{1,0:T(8,128)(2,1)S(1)}, u32[]{:S(2)}) copy-start(bf16[512,4096]{1,0:T(8,128)(2,1)S(1)} %get-tuple-element.9) | copy-start | bytes 12582916

commit v2 on v1

--- a/solution.py
+++ b/solution.py
@@ -13,14 +13,15 @@
 BF16, F32 = jnp.bfloat16, jnp.float32
 
 Z = 8
-Y_FIRST = (3, 3, 3, 3, 2, 2, 2, 0)
+Y_FIRST = (3, 3, 2, 2, 2, 2, 2, 2)
 
 EVENTS = (
-    "ag1", "L0", "ag2", "L1", "ag3", "L2", "L3", "zf0",
-    "YA0", "XA0", "L4", "YA1", "L5", "YA2", "XA1", "YB0", "L6", "zf1", "YA3", "XB0", "L7", "YA4", "XA2", "YB1",
-    "YA5", "YB2", "C0", "XA3", "XB1", "zf2", "YA6", "YB3", "XB2", "C1", "D0", "gi0", "gi1", "gi7",
-    "XA4", "XB3", "YB4", "C2", "D1", "zf3", "gi2", "gi6", "XA5", "YB5", "XB4", "C3", "D2", "XA6", "YB6", "XB5",
-    "C4", "D3", "gi3", "gi5", "zf4", "XA7", "XB6", "C5", "D4", "gi4", "C6", "D5", "XB7", "D6", "E", "C7", "F",
+    "La0", "Lb0", "La1", "Lb1", "ha0", "La2", "Lb2", "XA0", "YA0", "XA1", "La3", "Lb3", "hb0", "ha1", "YA1", "gi0",
+    "YA2", "XA2", "XB0", "La4", "Lb4", "YB0", "XB1", "hb1", "XA3", "gi1", "YA3", "gi7", "YB1", "YB2", "ha2", "XB2",
+    "XA4", "La5", "Lb5", "C0", "YA4", "C1", "hb2", "XB3", "D0", "YB3", "C2", "gi2", "XB4", "La6", "Lb6", "ha3",
+    "gi6", "YA5", "XA5", "YB4", "C3", "La7", "hb3", "Lb7", "YA6", "D1", "D2", "gi3", "YB5", "XA6", "XB5", "gi5",
+    "C4", "ha4", "YA7", "D3", "hb4", "YB6", "D4", "XB6", "XA7", "gi4", "C5", "YB7", "C6", "D5", "XB7", "D6", "C7",
+    "E", "F",
 )
 
 
@@ -70,10 +71,10 @@
 
     peers = [dev(y=up(y, 1, 4)), dev(y=up(y, -1, 4)), dev(y=up(y, 2, 4)), dev(xl=1 - xl), dev(c=1 - c),
              dev(z=up(z, 1, 8)), dev(z=up(z, -1, 8)), dev(xh=1 - xh), dev(xh=1 - xh, c=1 - c), dev(xh=1 - xh, xl=1 - xl)]
+    peers += [dev(y=up(y, d, 4), xl=1 - xl) for d in (1, 2, 3)]
     barrier = pltpu.get_barrier_semaphore()
     for peer in peers:
         pl.semaphore_signal(barrier, inc=1, device_id=peer, device_id_type=MESH)
-    pl.semaphore_wait(barrier, len(peers))
 
     def f32(ref):
         return ref[...].astype(F32)
@@ -106,41 +107,33 @@
         if hi > lo:
             lax.fori_loop(lo, hi, step, 0)
 
-    def leaf(s):
-        if s == 0:
+    def leaf(s, half):
+        if s == 0 and half == 0:
             cot_copy.wait()
-        for half in range(2):
-            load_in(s, half).wait()
-
-        def do_half(half):
-            T[...] = lax.dot_general(win[s, half], cot[...], (((0,), (0,)), ((), ())), preferred_element_type=F32)
-
-            def block(b):
-                rows = pl.ds(pl.multiple_of(b * 64, 64), 64)
-                q, pair = half * 2 + b // 2, (b % 2) * 2
-
-                def store(k, value):
-                    R[s, q, pl.ds(pair, 2), :, :, k * 128:(k + 1) * 128] = value.astype(BF16).reshape(2, 2, 16, 128)
-
-                quantize(lambda k: T[rows, k * 128:(k + 1) * 128], store, 64, unscale)
-
-            each(0, 4, block)
-
-            def send(q2):
-                q = half * 2 + q2
-
-                @pl.when(q < Y_FIRST[s])
-                def _():
-                    y_copy(s, q, 0).start()
-                    y_copy(s, q, 1).start()
-
-                @pl.when(q >= Y_FIRST[s])
-                def _():
-                    x_copy(s, q, 0).start()
-
-            each(0, 2, send)
-
-        each(0, 2, do_half)
+        load_in(s, half).wait()
+        T[...] = lax.dot_general(win[s, half], cot[...], (((0,), (0,)), ((), ())), preferred_element_type=F32)
+
+        def block(b):
+            rows = pl.ds(pl.multiple_of(b * 64, 64), 64)
+            q, pair = half * 2 + b // 2, (b % 2) * 2
+
+            def store(k, value):
+                R[s, q, pl.ds(pair, 2), :, :, k * 128:(k + 1) * 128] = value.astype(BF16).reshape(2, 2, 16, 128)
+
+            quantize(lambda k: T[rows, k * 128:(k + 1) * 128], store, 64, unscale)
+
+        each(0, 4, block)
+        if s == 0 and half == 0:
+            pl.semaphore_wait(barrier, len(peers))
+            w_copy.wait()
+            for i in range(7):
+                ag1(i).start()
+        for q in (half * 2, half * 2 + 1):
+            if q < Y_FIRST[s]:
+                y_copy(s, q, 0).start()
+                y_copy(s, q, 1).start()
+            else:
+                x_copy(s, q, 0).start()
 
     def y_forward(s):
         def body(q):
@@ -248,17 +241,14 @@
             total = total + f32(XB.at[i])
         gw[...] = total
 
-    def ag1(d):
+    def ag1(i):
         piece = W.at[z, xh, c, y, xl]
-        return to(piece, piece, ag_s.at[d - 1], ag_r.at[d - 1], dev(y=up(y, d, 4)))
-
-    def ag2():
-        piece = W.at[z, xh, c, :, xl]
-        return to(piece, piece, ag_s.at[3], ag_r.at[3], dev(xl=1 - xl))
+        dy, dx = (i + 1) // 2, (i + 1) % 2
+        return to(piece, piece, ag_s.at[i], ag_r.at[i], dev(y=up(y, dy, 4), xl=(xl + dx) % 2))
 
     def ag3():
         piece = W.at[z, xh, c]
-        return to(piece, piece, ag_s.at[4], ag_r.at[4], dev(xh=1 - xh, xl=1 - xl))
+        return to(piece, piece, ag_s.at[7], ag_r.at[7], dev(xh=1 - xh, xl=1 - xl))
 
     def ring(way, k, half):
         d = 1 - 2 * way
@@ -266,26 +256,39 @@
         i = way * 8 + (k - 1) * 2 + half
         return to(piece, piece, z_s.at[i], z_r.at[i], dev(z=up(z, d, 8)))
 
-    def ring_steps(k):
-        return [(way, k, half) for way in range(2) for half in range(2) if k < 4 or half == way]
-
-    def swap(i):
-        piece = W.at[up(z, -i, 8), :, c]
-        return to(piece, piece, cx_s.at[i], cx_r.at[i], dev(c=1 - c))
-
-    def hop(k):
+    def swap(i, half):
+        piece = W.at[up(z, -i, 8), half, c]
+        return to(piece, piece, cx_s.at[i * 2 + half], cx_r.at[i * 2 + half], dev(c=1 - c))
+
+    def hop(k, half):
+        if k == 0:
+            for way in range(2):
+                ring(way, 1, half).start()
+            swap(0, half).start()
+        elif k < 4:
+            for way in range(2):
+                ring(way, k, half).wait_recv()
+                if k < 3:
+                    ring(way, k + 1, half).start()
+            if k == 3:
+                ring(half, 4, half).start()
+            swap(k, half).start()
+            swap(8 - k, half).start()
+        else:
+            ring(half, 4, half).wait_recv()
+            swap(4, half).start()
+
+    def own_hop(k):
+        if k == 0:
+            for i in range(7):
+                ag1(i).wait_recv()
+            ag3().start()
+        hop(k, xh)
+
+    def other_hop(k):
         if k == 0:
             ag3().wait_recv()
-            for args in ring_steps(1):
-                ring(*args).start()
-            swap(0).start()
-            return
-        for way, _, half in ring_steps(k):
-            ring(way, k, half).wait_recv()
-            if k < 4 and (k < 3 or half == way):
-                ring(way, k + 1, half).start()
-        for i in ((k, 8 - k) if k < 4 else (4,)):
-            swap(i).start()
+        hop(k, 1 - xh)
 
     def put(i, slot):
         start = pl.multiple_of(up(z, -i, 8) * 512, 512)
@@ -294,7 +297,8 @@
     gi_done = []
 
     def grad_input(i):
-        swap(i).wait_recv()
+        swap(i, 0).wait_recv()
+        swap(i, 1).wait_recv()
         slot = len(gi_done) % 2
         if len(gi_done) >= 2:
             put(gi_done[-2], slot).wait()
@@ -309,23 +313,9 @@
         put(i, slot).start()
         gi_done.append(i)
 
-    def start_ag():
-        w_copy.wait()
-        for d in (1, 3, 2):
-            ag1(d).start()
-
-    def second_ag():
-        for d in (1, 3, 2):
-            ag1(d).wait_recv()
-        ag2().start()
-
-    def third_ag():
-        ag2().wait_recv()
-        ag3().start()
-
-    single = {"ag1": start_ag, "ag2": second_ag, "ag3": third_ag, "E": arrive, "F": finish}
-    numbered = {"L": leaf, "YA": y_forward, "XA": x_leaf, "YB": y_cross, "XB": x_forward, "C": close, "D": pass_on,
-                "zf": hop, "gi": grad_input}
+    single = {"E": arrive, "F": finish}
+    numbered = {"La": lambda s: leaf(s, 0), "Lb": lambda s: leaf(s, 1), "YA": y_forward, "XA": x_leaf, "YB": y_cross,
+                "XB": x_forward, "C": close, "D": pass_on, "ha": own_hop, "hb": other_hop, "gi": grad_input}
     for event in EVENTS:
         if event in single:
             single[event]()
@@ -336,15 +326,15 @@
         put(i, gi_done.index(i) % 2).wait()
     for s in range(8):
         pltpu.make_async_copy(RB.at[s], RB.at[s], s_sem.at[s]).wait()
-    for d in (1, 3, 2):
-        ag1(d).wait_send()
-    ag2().wait_send()
+    for i in range(7):
+        ag1(i).wait_send()
     ag3().wait_send()
-    for k in range(1, 5):
-        for args in ring_steps(k):
-            ring(*args).wait_send()
-    for i in range(8):
-        swap(i).wait_send()
+    for half in range(2):
+        for way in range(2):
+            for k in range(1, 5 if way == half else 4):
+                ring(way, k, half).wait_send()
+        for i in range(8):
+            swap(i, half).wait_send()
     for s in range(7):
         g_copy(s).wait_send()
         for half in range(2 if s == 0 else 1):
@@ -353,14 +343,28 @@
         last_copy(i).wait_send()
 
 
+def deliver(sums, products, grad_weight, grad_input, sem):
+    copies = [pltpu.make_async_copy(products.at[pl.ds(i * 64, 64)], grad_input.at[pl.ds(i * 64, 64)], sem.at[i])
+              for i in range(8)]
+    for copy in copies:
+        copy.start()
+    for row in range(16):
+        start = row % 2 * 1024
+        grad_weight[row // 2:row // 2 + 1, start:start + 1024] = sums[row:row + 1, :]
+    for copy in copies:
+        copy.wait()
+
+
 def local(unscale, inputs, cotangent, weight):
     dma = pltpu.SemaphoreType.DMA
-    hbm = pl.BlockSpec(memory_space=pl.ANY)
-    grad_weight, grad_input = pl.pallas_call(
+    hbm = pl.BlockSpec(memory_space=pltpu.HBM)
+    anywhere = pl.BlockSpec(memory_space=pl.ANY)
+    vmem = pl.BlockSpec(memory_space=pltpu.VMEM)
+    sums, products = pl.pallas_call(
         lambda *refs: kernel(unscale, *refs),
         out_shape=(jax.ShapeDtypeStruct((16, 1024), F32), jax.ShapeDtypeStruct((512, 4096), BF16)),
         in_specs=[hbm] * 3,
-        out_specs=(pl.BlockSpec(memory_space=pltpu.VMEM), hbm),
+        out_specs=(vmem, anywhere),
         scratch_shapes=[
             pltpu.VMEM((512, 1024), BF16),
             pltpu.VMEM((8, 2, 512, 256), BF16),
@@ -376,14 +380,22 @@
             pltpu.VMEM((4, 16, 1024), BF16),
             pltpu.VMEM((2, 512, 512), BF16),
             dma((9, 2)), dma((8,)), dma((8, 4, 4)),
-            dma((5,)), dma((5,)), dma((16,)), dma((16,)), dma((8,)), dma((8,)),
+            dma((8,)), dma((8,)), dma((16,)), dma((16,)), dma((16,)), dma((16,)),
             dma((7,)), dma((7,)), dma((8,)), dma((8,)), dma((4,)), dma((4,)), dma((2,)),
         ],
         compiler_params=pltpu.CompilerParams(collective_id=0, has_side_effects=True, vmem_limit_bytes=48 << 20),
         cost_estimate=pl.CostEstimate(flops=4 * 512 * 4096 * 1024, bytes_accessed=10 << 20, transcendentals=0),
         name="exchange",
     )(inputs, cotangent, weight)
-    return grad_weight.reshape(8, 2048), grad_input
+    return pl.pallas_call(
+        deliver,
+        out_shape=(jax.ShapeDtypeStruct((8, 2048), F32), jax.ShapeDtypeStruct((512, 4096), BF16)),
+        in_specs=[vmem, vmem],
+        out_specs=(vmem, hbm),
+        scratch_shapes=[dma((8,))],
+        compiler_params=pltpu.CompilerParams(vmem_limit_bytes=16 << 20),
+        name="deliver",
+    )(sums, products)
 
 
 def solution(mesh):

time: 103 us -> 81.5 us (0.79)
  Pallas kernels: 92.8 us -> 78.7 us
  local copies, waits for them, and re-layouts: 9.26 us -> 1.98 us
    pallas_call x1, Pallas kernels: 92.8 us -> 76 us  [local(): pl.pallas_call(lambda *refs: kernel(unscale, *refs), out_shape=(jax.Shape...]
    unnamed x7 -> x4, local copies, waits for them, and re-layouts: 8.61 us -> 1.98 us
    pallas_call x0 -> x1, Pallas kernels: none -> 2.7 us  [local(): pl.pallas_call(deliver, out_shape=(jax.ShapeDtypeStruct((8, 2048), F32),...]
where the time goes in v2:
time: 81.5 us; the launch traced here: 81.3 us
  Pallas kernels  78.7 us (97%)
  local copies, waits for them, and re-layouts  1.98 us (2%)
    pallas_call x1, Pallas kernels, local(): pl.pallas_call(lambda *refs: kernel(unscale, *refs), out_shape=(jax.Shape...  76 us
    pallas_call x1, Pallas kernels, local(): pl.pallas_call(deliver, out_shape=(jax.ShapeDtypeStruct((8, 2048), F32),...  2.7 us
    unnamed x4, local copies, waits for them, and re-layouts  1.98 us

profile of v2, /device:TPU:1, one launch (start us, length us, event | category | flops | bytes accessed | tf_op | source)
XLA Modules:
  0.0 81.3 jit_solution(1882702696700941239)
XLA Ops:
  0.6 0.0 copy-start
  0.6 1.2 %copy-done = bf16[512,1024]{1,0:T(8,128)(2,1)S(1)} copy-done((bf16[512,1024]{1,0:T(8,128)(2,1)S(1)}, bf16[512,1024]{1,0:T(8,128)(2,1)}, u32[]{:S(2)}) %copy-start) | copy-done | bytes 1048600
  1.9 0.0 copy-start.1
  1.9 0.8 copy-done.1
  2.6 76.0 %exchange.1 = (f32[16,1024]{1,0:T(8,128)S(1)}, bf16[512,4096]{1,0:T(8,128)(2,1)S(1)}) custom-call(bf16[512,4096]{1,0:T(8,128)(2,1)} %refs_0_.1, bf16[512,1024]{1,0:T(8,128)(2,1)S(1)} %copy-done, bf16[16,1024]{1,0:T(8,128)(2,1)S(1)} %copy-done.1), custom_call_target="tpu_custom_call" | custom-call | flops 8589934592 | bytes 10485760 | tf_op jit(solution)/shard_map/exchange/pallas_call | solution.py:363
  78.6 2.7 %deliver.1 = (f32[8,2048]{1,0:T(8,128)}, bf16[512,4096]{1,0:T(8,128)(2,1)}) custom-call(f32[16,1024]{1,0:T(8,128)S(1)} %get-tuple-element.4.sums, bf16[512,4096]{1,0:T(8,128)(2,1)S(1)} %get-tuple-element.5.products), custom_call_target="tpu_custom_call" | custom-call | tf_op jit(solution)/shard_map/deliver/pallas_call | solution.py:390
Async XLA Ops:
  0.6 1.2 %copy-start = (bf16[512,1024]{1,0:T(8,128)(2,1)S(1)}, bf16[512,1024]{1,0:T(8,128)(2,1)}, u32[]{:S(2)}) copy-start(bf16[512,1024]{1,0:T(8,128)(2,1)} %refs_1_.1) | copy-start | bytes 3145732
  1.9 0.8 copy-start.1

commit v3 on v2

--- a/solution.py
+++ b/solution.py
@@ -13,15 +13,16 @@
 BF16, F32 = jnp.bfloat16, jnp.float32
 
 Z = 8
-Y_FIRST = (3, 3, 2, 2, 2, 2, 2, 2)
+FAR = 3
+Y_FIRST = (3, 2, 2, 2, 2, 2, 2, 2)
 
 EVENTS = (
-    "La0", "Lb0", "La1", "Lb1", "ha0", "La2", "Lb2", "XA0", "YA0", "XA1", "La3", "Lb3", "hb0", "ha1", "YA1", "gi0",
-    "YA2", "XA2", "XB0", "La4", "Lb4", "YB0", "XB1", "hb1", "XA3", "gi1", "YA3", "gi7", "YB1", "YB2", "ha2", "XB2",
-    "XA4", "La5", "Lb5", "C0", "YA4", "C1", "hb2", "XB3", "D0", "YB3", "C2", "gi2", "XB4", "La6", "Lb6", "ha3",
-    "gi6", "YA5", "XA5", "YB4", "C3", "La7", "hb3", "Lb7", "YA6", "D1", "D2", "gi3", "YB5", "XA6", "XB5", "gi5",
-    "C4", "ha4", "YA7", "D3", "hb4", "YB6", "D4", "XB6", "XA7", "gi4", "C5", "YB7", "C6", "D5", "XB7", "D6", "C7",
-    "E", "F",
+    "AG", "Lb0", "La3", "Lb2", "A2", "La0", "Lb1", "La2", "Lb3", "La1", "ha0", "YA0", "La4", "ha1", "Lb4", "YA1",
+    "hb0", "XA1", "XA0", "YB0", "Lb6", "XA3", "XA2", "YA3", "XB0", "YA2", "XB1", "La6", "XA4", "ha2", "La5", "YB1",
+    "La7", "Lb5", "YB2", "hb1", "XB2", "YA6", "gi0", "C0", "C1", "ha3", "YA4", "XB3", "Lb7", "YA5", "YB3", "hb2",
+    "D0", "XA5", "gi1", "XA6", "XB4", "YB4", "C2", "YA7", "gi6", "ha4", "YB6", "D2", "D1", "YB5", "XA7", "gi7",
+    "XB5", "C3", "XB6", "C4", "hb3", "YB7", "D3", "XB7", "D4", "gi2", "C5", "C6", "C7", "D5", "hb4", "D6", "gi5",
+    "gi3", "gi4", "F",
 )
 
 
@@ -39,8 +40,8 @@
         store(k, code * scale)
 
 
-def kernel(unscale, inp, cot_hbm, w_hbm, gw, gi, cot, win, T, R, RB, W, F, G, CB, ZB, EB, XB, GS,
-           in_sem, s_sem, r_sem, ag_s, ag_r, z_s, z_r, cx_s, cx_r, g_s, g_r, zs_s, zs_r, xb_s, xb_r, gi_sem):
+def kernel(unscale, inp, cot_hbm, w_hbm, gw, gi, cot, win, T, R, RB, W, F, G, CB, ZB, XB, GS,
+           in_sem, s_sem, r_sem, ag_s, ag_r, ac_s, ac_r, z_s, z_r, cx_s, cx_r, g_s, g_r, zs_s, zs_r, xb_s, xb_r, gi_sem):
     node, loc = lax.axis_index("node"), lax.axis_index("local")
     z, xh, c, y, xl = node // 4, (node // 2) % 2, node % 2, loc // 2, loc % 2
 
@@ -65,13 +66,13 @@
     w_copy = pltpu.make_async_copy(w_hbm, W.at[z, xh, c, y, xl], in_sem.at[8, 1])
     w_copy.start()
     cot_copy.start()
-    for s in range(8):
-        for half in range(2):
-            load_in(s, half).start()
+    for event in EVENTS:
+        if event[:2] in ("La", "Lb"):
+            load_in(int(event[2]), "ab".index(event[1])).start()
 
     peers = [dev(y=up(y, 1, 4)), dev(y=up(y, -1, 4)), dev(y=up(y, 2, 4)), dev(xl=1 - xl), dev(c=1 - c),
              dev(z=up(z, 1, 8)), dev(z=up(z, -1, 8)), dev(xh=1 - xh), dev(xh=1 - xh, c=1 - c), dev(xh=1 - xh, xl=1 - xl)]
-    peers += [dev(y=up(y, d, 4), xl=1 - xl) for d in (1, 2, 3)]
+    peers += [dev(z=up(z, d, 8), xh=1 - xh) for d in (1, -1)]
     barrier = pltpu.get_barrier_semaphore()
     for peer in peers:
         pl.semaphore_signal(barrier, inc=1, device_id=peer, device_id_type=MESH)
@@ -108,8 +109,6 @@
             lax.fori_loop(lo, hi, step, 0)
 
     def leaf(s, half):
-        if s == 0 and half == 0:
-            cot_copy.wait()
         load_in(s, half).wait()
         T[...] = lax.dot_general(win[s, half], cot[...], (((0,), (0,)), ((), ())), preferred_element_type=F32)
 
@@ -123,11 +122,6 @@
             quantize(lambda k: T[rows, k * 128:(k + 1) * 128], store, 64, unscale)
 
         each(0, 4, block)
-        if s == 0 and half == 0:
-            pl.semaphore_wait(barrier, len(peers))
-            w_copy.wait()
-            for i in range(7):
-                ag1(i).start()
         for q in (half * 2, half * 2 + 1):
             if q < Y_FIRST[s]:
                 y_copy(s, q, 0).start()
@@ -174,7 +168,7 @@
         return to(G.at[s, :, 1 - c], CB.at[s], g_s.at[s], g_r.at[s], dev(c=1 - c))
 
     last = [(G.at[7, xh, 1 - c], dev(c=1 - c)), (G.at[7, 1 - xh, c], dev(xh=1 - xh)),
-            (G.at[7, 1 - xh, 1 - c], dev(xh=1 - xh, c=1 - c)), (EB.at[1 - xh], dev(xh=1 - xh))]
+            (G.at[7, 1 - xh, 1 - c], dev(xh=1 - xh, c=1 - c))]
 
     def last_copy(i):
         return to(last[i][0], XB.at[i], xb_s.at[i], xb_r.at[i], last[i][1])
@@ -201,14 +195,21 @@
         if s < 7:
             g_copy(s).start()
         else:
-            for i in range(3):
+            for i in (2, 1, 0):
                 last_copy(i).start()
 
-    def z_copy(s, half=0):
-        right, left = dev(z=up(z, 1, 8)), dev(z=up(z, -1, 8))
+    def z_copy(s, part=0):
+        i = s + 7 * part
+        target = up(z, 1, 8) if s % 2 or (s == 0 and part == 0) else up(z, -1, 8)
         if s == 0:
-            return to(G.at[0, half, c], ZB.at[0, half], zs_s.at[7 * half], zs_r.at[7 * half], left if half else right)
-        return to(G.at[s, :, c], ZB.at[s], zs_s.at[s], zs_r.at[s], right if s % 2 else left)
+            return to(G.at[0, part, c], ZB.at[0, part], zs_s.at[i], zs_r.at[i], dev(z=target))
+        if s < 5:
+            return to(G.at[s, :, c], ZB.at[s], zs_s.at[i], zs_r.at[i], dev(z=target))
+        half = (1 - xh) if part else xh
+        return to(G.at[s, half, c], ZB.at[s, part], zs_s.at[i], zs_r.at[i], dev(z=target, xh=half))
+
+    def z_parts(s):
+        return (0,) if 1 <= s < 5 else (1, 0)
 
     def pass_on(s):
         g_copy(s).wait_recv()
@@ -224,31 +225,24 @@
             elif s - 1 == half:
                 total = total + f32(ZB.at[0, half])
             own[...] = total.astype(BF16)
-        for half in range(2 if s == 0 else 1):
-            z_copy(s, half).start()
-
-    def arrive():
-        z_copy(5).wait_recv()
-        z_copy(6).wait_recv()
-        EB[...] = (f32(ZB.at[5]) + f32(ZB.at[6])).astype(BF16)
-        last_copy(3).start()
+        for part in z_parts(s):
+            z_copy(s, part).start()
 
     def finish():
-        for i in range(4):
+        total = f32(G.at[7, xh, c])
+        for s in (5, 6):
+            for part in (0, 1):
+                z_copy(s, part).wait_recv()
+                total = total + f32(ZB.at[s, part])
+        for i in range(3):
             last_copy(i).wait_recv()
-        total = f32(G.at[7, xh, c]) + f32(ZB.at[5, xh]) + f32(ZB.at[6, xh])
-        for i in range(4):
             total = total + f32(XB.at[i])
         gw[...] = total
 
-    def ag1(i):
-        piece = W.at[z, xh, c, y, xl]
-        dy, dx = (i + 1) // 2, (i + 1) % 2
-        return to(piece, piece, ag_s.at[i], ag_r.at[i], dev(y=up(y, dy, 4), xl=(xl + dx) % 2))
-
-    def ag3():
-        piece = W.at[z, xh, c]
-        return to(piece, piece, ag_s.at[7], ag_r.at[7], dev(xh=1 - xh, xl=1 - xl))
+    def ag1(i, whose=0):
+        piece = W.at[z, xh, c, y, (xl + whose) % 2]
+        sems = ag_s.at[whose * 4 + i], ag_r.at[whose * 4 + i]
+        return to(piece, piece, *sems, dev(y=up(y, i, 4), xl=(xl + (i == 0)) % 2))
 
     def ring(way, k, half):
         d = 1 - 2 * way
@@ -260,35 +254,50 @@
         piece = W.at[up(z, -i, 8), half, c]
         return to(piece, piece, cx_s.at[i * 2 + half], cx_r.at[i * 2 + half], dev(c=1 - c))
 
-    def hop(k, half):
+    def across(i):
+        piece = W.at[up(z, -i, 8), xh, c]
+        return to(piece, piece, ac_s.at[i], ac_r.at[i], dev(xh=1 - xh, xl=1 - xl))
+
+    def from_across(i):
+        piece = W.at[up(z, -i, 8), 1 - xh, c]
+        to(piece, piece, ac_s.at[i], ac_r.at[i], dev(xh=1 - xh, xl=1 - xl)).wait_recv()
+
+    def spots(k):
+        return (k, 8 - k) if 0 < k < 4 else (k,)
+
+    def own_hop(k):
         if k == 0:
+            for whose in range(2):
+                for i in (1, 3, 2):
+                    ag1(i, whose).wait_recv()
             for way in range(2):
-                ring(way, 1, half).start()
-            swap(0, half).start()
+                ring(way, 1, xh).start()
         elif k < 4:
             for way in range(2):
-                ring(way, k, half).wait_recv()
+                ring(way, k, xh).wait_recv()
                 if k < 3:
-                    ring(way, k + 1, half).start()
+                    ring(way, k + 1, xh).start()
             if k == 3:
-                ring(half, 4, half).start()
-            swap(k, half).start()
-            swap(8 - k, half).start()
+                ring(c, 4, xh).start()
         else:
-            ring(half, 4, half).wait_recv()
-            swap(4, half).start()
-
-    def own_hop(k):
-        if k == 0:
-            for i in range(7):
-                ag1(i).wait_recv()
-            ag3().start()
-        hop(k, xh)
+            ring(c, 4, xh).wait_recv()
+        for i in spots(k):
+            if k == 0 or k >= FAR:
+                across(i).start()
+            swap(i, xh).start()
 
     def other_hop(k):
-        if k == 0:
-            ag3().wait_recv()
-        hop(k, 1 - xh)
+        if k == 0 or k >= FAR:
+            for i in spots(k):
+                from_across(i)
+        else:
+            for way in range(2):
+                ring(way, k, 1 - xh).wait_recv()
+        if k + 1 < FAR:
+            for way in range(2):
+                ring(way, k + 1, 1 - xh).start()
+        for i in spots(k):
+            swap(i, 1 - xh).start()
 
     def put(i, slot):
         start = pl.multiple_of(up(z, -i, 8) * 512, 512)
@@ -313,7 +322,19 @@
         put(i, slot).start()
         gi_done.append(i)
 
-    single = {"E": arrive, "F": finish}
+    def open_up():
+        pl.semaphore_wait(barrier, len(peers))
+        w_copy.wait()
+        for i in (0, 2, 1, 3):
+            ag1(i).start()
+        cot_copy.wait()
+
+    def second_ag():
+        ag1(0).wait_recv()
+        for i in (2, 1, 3):
+            ag1(i, 1).start()
+
+    single = {"AG": open_up, "A2": second_ag, "F": finish}
     numbered = {"La": lambda s: leaf(s, 0), "Lb": lambda s: leaf(s, 1), "YA": y_forward, "XA": x_leaf, "YB": y_cross,
                 "XB": x_forward, "C": close, "D": pass_on, "ha": own_hop, "hb": other_hop, "gi": grad_input}
     for event in EVENTS:
@@ -326,20 +347,25 @@
         put(i, gi_done.index(i) % 2).wait()
     for s in range(8):
         pltpu.make_async_copy(RB.at[s], RB.at[s], s_sem.at[s]).wait()
-    for i in range(7):
-        ag1(i).wait_send()
-    ag3().wait_send()
-    for half in range(2):
+    for whose in range(2):
+        for i in range(whose, 4):
+            ag1(i, whose).wait_send()
+    for i in range(8):
+        for half in range(2):
+            swap(i, half).wait_send()
+    for i in (0,) + tuple(range(FAR, 9 - FAR)):
+        across(i).wait_send()
+    for k in range(1, 4):
         for way in range(2):
-            for k in range(1, 5 if way == half else 4):
-                ring(way, k, half).wait_send()
-        for i in range(8):
-            swap(i, half).wait_send()
+            ring(way, k, xh).wait_send()
+            if k < FAR:
+                ring(way, k, 1 - xh).wait_send()
+    ring(c, 4, xh).wait_send()
     for s in range(7):
         g_copy(s).wait_send()
-        for half in range(2 if s == 0 else 1):
-            z_copy(s, half).wait_send()
-    for i in range(4):
+        for part in z_parts(s):
+            z_copy(s, part).wait_send()
+    for i in range(3):
         last_copy(i).wait_send()
 
 
@@ -376,17 +402,16 @@
             pltpu.VMEM((8, 2, 2, 16, 1024), BF16),
             pltpu.VMEM((7, 2, 16, 1024), BF16),
             pltpu.VMEM((7, 2, 16, 1024), BF16),
-            pltpu.VMEM((2, 16, 1024), BF16),
-            pltpu.VMEM((4, 16, 1024), BF16),
+            pltpu.VMEM((3, 16, 1024), BF16),
             pltpu.VMEM((2, 512, 512), BF16),
             dma((9, 2)), dma((8,)), dma((8, 4, 4)),
-            dma((8,)), dma((8,)), dma((16,)), dma((16,)), dma((16,)), dma((16,)),
-            dma((7,)), dma((7,)), dma((8,)), dma((8,)), dma((4,)), dma((4,)), dma((2,)),
+            dma((8,)), dma((8,)), dma((8,)), dma((8,)), dma((16,)), dma((16,)), dma((16,)), dma((16,)),
+            dma((7,)), dma((7,)), dma((14,)), dma((14,)), dma((3,)), dma((3,)), dma((2,)),
         ],
         compiler_params=pltpu.CompilerParams(collective_id=0, has_side_effects=True, vmem_limit_bytes=48 << 20),
         cost_estimate=pl.CostEstimate(flops=4 * 512 * 4096 * 1024, bytes_accessed=10 << 20, transcendentals=0),
         name="exchange",
-    )(inputs, cotangent, weight)
+    )(*[pltpu.with_memory_space_constraint(array, pltpu.HBM) for array in (inputs, cotangent, weight)])
     return pl.pallas_call(
         deliver,
         out_shape=(jax.ShapeDtypeStruct((8, 2048), F32), jax.ShapeDtypeStruct((512, 4096), BF16)),

time: 81.5 us -> 78.6 us (0.964)
  local copies, waits for them, and re-layouts: 1.98 us -> 0 us
    unnamed x4 -> x0, local copies, waits for them, and re-layouts: 1.98 us -> none
where the time goes in v3:
time: 78.6 us; the launch traced here: 78.5 us
  Pallas kernels  77.9 us (99%)
    pallas_call x1, Pallas kernels, local(): pl.pallas_call(lambda *refs: kernel(unscale, *refs), out_shape=(jax.Shape...  75.2 us
    pallas_call x1, Pallas kernels, local(): pl.pallas_call(deliver, out_shape=(jax.ShapeDtypeStruct((8, 2048), F32),...  2.7 us

profile of v3, /device:TPU:1, one launch (start us, length us, event | category | flops | bytes accessed | tf_op | source)
XLA Modules:
  0.0 78.5 jit_solution(17807266487449613604)
XLA Ops:
  0.6 75.2 %exchange.1 = (f32[16,1024]{1,0:T(8,128)S(1)}, bf16[512,4096]{1,0:T(8,128)(2,1)S(1)}) custom-call(bf16[512,4096]{1,0:T(8,128)(2,1)} %refs_0_.1, bf16[512,1024]{1,0:T(8,128)(2,1)} %refs_1_.1, bf16[16,1024]{1,0:T(8,128)(2,1)} %refs_2_.1), custom_call_target="tpu_custom_call" | custom-call | flops 8589934592 | bytes 10485760 | tf_op jit(solution)/shard_map/exchange/pallas_call | solution.py:389
  75.8 2.7 %deliver.1 = (f32[8,2048]{1,0:T(8,128)}, bf16[512,4096]{1,0:T(8,128)(2,1)}) custom-call(f32[16,1024]{1,0:T(8,128)S(1)} %get-tuple-element.4.sums, bf16[512,4096]{1,0:T(8,128)(2,1)S(1)} %get-tuple-element.5.products), custom_call_target="tpu_custom_call" | custom-call | tf_op jit(solution)/shard_map/deliver/pallas_call | solution.py:415

commit v4 on v3

--- a/solution.py
+++ b/solution.py
@@ -62,20 +62,20 @@
         start = pl.multiple_of(slot_z(s) * 512 + half * 256, 256)
         return pltpu.make_async_copy(inp.at[:, pl.ds(start, 256)], win.at[s, half], in_sem.at[s, half])
 
-    cot_copy = pltpu.make_async_copy(cot_hbm, cot, in_sem.at[8, 0])
-    w_copy = pltpu.make_async_copy(w_hbm, W.at[z, xh, c, y, xl], in_sem.at[8, 1])
-    w_copy.start()
-    cot_copy.start()
-    for event in EVENTS:
-        if event[:2] in ("La", "Lb"):
-            load_in(int(event[2]), "ab".index(event[1])).start()
-
     peers = [dev(y=up(y, 1, 4)), dev(y=up(y, -1, 4)), dev(y=up(y, 2, 4)), dev(xl=1 - xl), dev(c=1 - c),
              dev(z=up(z, 1, 8)), dev(z=up(z, -1, 8)), dev(xh=1 - xh), dev(xh=1 - xh, c=1 - c), dev(xh=1 - xh, xl=1 - xl)]
     peers += [dev(z=up(z, d, 8), xh=1 - xh) for d in (1, -1)]
     barrier = pltpu.get_barrier_semaphore()
     for peer in peers:
         pl.semaphore_signal(barrier, inc=1, device_id=peer, device_id_type=MESH)
+
+    cot_copies = [pltpu.make_async_copy(cot_hbm.at[pl.ds(i * 128, 128)], cot.at[pl.ds(i * 128, 128)], in_sem.at[9 + i // 2, i % 2])
+                  for i in range(4)]
+    w_copy = pltpu.make_async_copy(w_hbm, W.at[z, xh, c, y, xl], in_sem.at[8, 1])
+    w_copy.start()
+    leaves = [load_in(int(event[2]), "ab".index(event[1])) for event in EVENTS if event[:2] in ("La", "Lb")]
+    for copy in cot_copies + leaves[:2]:
+        copy.start()
 
     def f32(ref):
         return ref[...].astype(F32)
@@ -327,7 +327,10 @@
         w_copy.wait()
         for i in (0, 2, 1, 3):
             ag1(i).start()
-        cot_copy.wait()
+        for copy in leaves[2:]:
+            copy.start()
+        for copy in cot_copies:
+            copy.wait()
 
     def second_ag():
         ag1(0).wait_recv()
@@ -404,7 +407,7 @@
             pltpu.VMEM((7, 2, 16, 1024), BF16),
             pltpu.VMEM((3, 16, 1024), BF16),
             pltpu.VMEM((2, 512, 512), BF16),
-            dma((9, 2)), dma((8,)), dma((8, 4, 4)),
+            dma((11, 2)), dma((8,)), dma((8, 4, 4)),
             dma((8,)), dma((8,)), dma((8,)), dma((8,)), dma((16,)), dma((16,)), dma((16,)), dma((16,)),
             dma((7,)), dma((7,)), dma((14,)), dma((14,)), dma((3,)), dma((3,)), dma((2,)),
         ],

time: 78.6 us -> 78.6 us (level)
  no operation moved by 1% of the time
where the time goes in v4:
time: 78.6 us; the launch traced here: 78.5 us
  Pallas kernels  77.9 us (99%)
    pallas_call x1, Pallas kernels, local(): pl.pallas_call(lambda *refs: kernel(unscale, *refs), out_shape=(jax.Shape...  75.2 us
    pallas_call x1, Pallas kernels, local(): pl.pallas_call(deliver, out_shape=(jax.ShapeDtypeStruct((8, 2048), F32),...  2.7 us

profile of v4, /device:TPU:1, one launch (start us, length us, event | category | flops | bytes accessed | tf_op | source)
XLA Modules:
  0.0 78.5 jit_solution(8723510003656381346)
XLA Ops:
  0.6 75.2 %exchange.1 = (f32[16,1024]{1,0:T(8,128)S(1)}, bf16[512,4096]{1,0:T(8,128)(2,1)S(1)}) custom-call(bf16[512,4096]{1,0:T(8,128)(2,1)} %refs_0_.1, bf16[512,1024]{1,0:T(8,128)(2,1)} %refs_1_.1, bf16[16,1024]{1,0:T(8,128)(2,1)} %refs_2_.1), custom_call_target="tpu_custom_call" | custom-call | flops 8589934592 | bytes 10485760 | tf_op jit(solution)/shard_map/exchange/pallas_call | solution.py:392
  75.8 2.7 %deliver.1 = (f32[8,2048]{1,0:T(8,128)}, bf16[512,4096]{1,0:T(8,128)(2,1)}) custom-call(f32[16,1024]{1,0:T(8,128)S(1)} %get-tuple-element.4.sums, bf16[512,4096]{1,0:T(8,128)(2,1)S(1)} %get-tuple-element.5.products), custom_call_target="tpu_custom_call" | custom-call | tf_op jit(solution)/shard_map/deliver/pallas_call | solution.py:418

commit v5 on v4

--- a/solution.py
+++ b/solution.py
@@ -13,7 +13,7 @@
 BF16, F32 = jnp.bfloat16, jnp.float32
 
 Z = 8
-FAR = 3
+FAR = 2
 Y_FIRST = (3, 2, 2, 2, 2, 2, 2, 2)
 
 EVENTS = (

time: 78.6 us -> 78.8 us (level)
  no operation moved by 1% of the time
where the time goes in v5:
time: 78.8 us; the launch traced here: 78.7 us
  Pallas kernels  78.1 us (99%)
    pallas_call x1, Pallas kernels, local(): pl.pallas_call(lambda *refs: kernel(unscale, *refs), out_shape=(jax.Shape...  75.4 us
    pallas_call x1, Pallas kernels, local(): pl.pallas_call(deliver, out_shape=(jax.ShapeDtypeStruct((8, 2048), F32),...  2.7 us

profile of v5, /device:TPU:1, one launch (start us, length us, event | category | flops | bytes accessed | tf_op | source)
XLA Modules:
  0.0 78.7 jit_solution(6898010526522103137)
XLA Ops:
  0.6 75.4 %exchange.1 = (f32[16,1024]{1,0:T(8,128)S(1)}, bf16[512,4096]{1,0:T(8,128)(2,1)S(1)}) custom-call(bf16[512,4096]{1,0:T(8,128)(2,1)} %refs_0_.1, bf16[512,1024]{1,0:T(8,128)(2,1)} %refs_1_.1, bf16[16,1024]{1,0:T(8,128)(2,1)} %refs_2_.1), custom_call_target="tpu_custom_call" | custom-call | flops 8589934592 | bytes 10485760 | tf_op jit(solution)/shard_map/exchange/pallas_call | solution.py:392
  76.0 2.7 %deliver.1 = (f32[8,2048]{1,0:T(8,128)}, bf16[512,4096]{1,0:T(8,128)(2,1)}) custom-call(f32[16,1024]{1,0:T(8,128)S(1)} %get-tuple-element.4.sums, bf16[512,4096]{1,0:T(8,128)(2,1)S(1)} %get-tuple-element.5.products), custom_call_target="tpu_custom_call" | custom-call | tf_op jit(solution)/shard_map/deliver/pallas_call | solution.py:418
